TPU v7x, 32 devices: a whole 2x2x4 slice. The times are simulated.
32 devices in a mesh: gx: 8 (over y, x, core), gy: 4 (over z).
Axes of the slice: x: 2, y: 2, z: 4, core: 2. Of those that a mesh axis runs over, the one named last changes fastest.
Arguments:
- fields: bfloat16 [10, 32, 512, 512], P(None, None, 'gx', 'gy'), as said below
- dense_list: int32 [4, 8, 10], replicated, may hold values from -1 to 63, as said below
- filter_device: int32 [4, 8, 10], replicated, may hold values from -1 to 7, as said below
- pencil_order: int32 [16], replicated, may hold values from 0 to 15, each once
Outputs:
- tile_stats: float32 [128, 2048], P(('gx', 'gy'))
- coarse_closure: float32 [16, 512], P('gy')
Inputs may be any that keep to these rules, and one draw needn't show every extreme that they name: `dense_list`: row [gy, gx] lists distinct local tile indices of device (gx, gy), its listed entries first and -1 after them; in every gy row the busiest device lists 10 tiles and some list only a few. `filter_device`: -1 exactly where dense_list is -1; within a gy row each gx index receives exactly 4 listed tiles and at most 2 from any one listing device, and that most is met. `fields`: channel 0 lies between 0.05 and 0.6; channels 8 and 9 are positive.
All inputs are finite; a program needn't handle non-finite values.
Results may differ from a plain program's by a relative error of at most 0.0003.
Values may be sent and summed in bfloat16 or wider, within the bound.
A program may use at most 192 MiB of HBM per device.

v0:
```python
import functools

import jax
import jax.numpy as jnp
import numpy as np
from jax import lax
from jax.experimental import pallas as pl
from jax.experimental.pallas import tpu as pltpu
from jax.sharding import PartitionSpec as P

TE = 16
HW = 4
CAP = 2
SPAN = TE + 2 * HW
BF = jnp.bfloat16
F32 = jnp.float32
MESH = pl.DeviceIdType.MESH


def dot(a, b):
    return lax.dot_general(a, b, (((1,), (0,)), ((), ())), preferred_element_type=F32)


def window_weights():
    z = np.arange(SPAN)[:, None, None, None]
    w = np.arange(32)[None, :, None, None]
    zo = np.arange(TE)[None, None, :, None]
    yo = np.arange(TE)[None, None, None, :]
    out = []
    for k in range(1, HW + 1):
        m = (np.abs(z - HW - zo) <= k) & (np.abs(w - HW - yo) <= k)
        m = m.reshape(SPAN * 32, TE * TE)
        out.append(np.concatenate([m, m], axis=0))
    return np.stack(out).astype(jnp.bfloat16)


def block_weights():
    par = np.arange(2)[:, None, None, None]
    bx = np.arange(4)[None, :, None, None]
    h = np.arange(2)[None, None, :, None]
    lane = np.arange(128)[None, None, None, :]
    plane = h * 128 + lane
    target = par * 64 + (plane // TE // 4) * 16 + bx * 4 + (plane % TE) // 4
    target = target.reshape(-1)
    m = (target[:, None] == np.arange(128)[None, :]) / 64.0
    return np.concatenate([m, m], axis=0).astype(jnp.bfloat16)


def edge_weights(nz):
    z = np.arange(nz)[:, None, None, None]
    r = np.arange(HW)[None, :, None, None]
    zs = np.arange(nz)[None, None, :, None]
    s = np.arange(16)[None, None, None, :]
    last = ((z == zs) & (s == 12 + r)).reshape(nz * HW, nz * 16)
    first = ((z == zs) & (s == r)).reshape(nz * HW, nz * 16)
    take = np.stack([last, first])
    give = np.stack([last.T, first.T])
    return take.astype(jnp.bfloat16), give.astype(jnp.bfloat16)


def column_weights(nz, ny):
    z = np.arange(nz)[:, None, None, None]
    y = np.arange(ny)[None, :, None, None]
    side = np.arange(2)[None, None, :, None]
    lane = np.arange(128)[None, None, None, :]
    low = (side == 0) & (y >= ny - HW) & (lane == z * HW + y - (ny - HW))
    high = (side == 1) & (y < HW) & (lane == z * HW + y)
    return (low | high).reshape(nz // 2, 2 * ny, 256).astype(jnp.bfloat16)


def halo_kernel(
    gxn, gyn, f_ref, take_ref, give_ref, col_ref, p_ref, yh_ref, sx, rx, sy, ssem, rsem
):
    nc, nz, nx, ny = f_ref.shape
    px = nx + 32
    gx, gy = lax.axis_index("gx"), lax.axis_index("gy")
    right = (lax.rem(gx + 1, gxn), gy)
    left = (lax.rem(gx + gxn - 1, gxn), gy)
    up = (gx, lax.rem(gy + 1, gyn))
    down = (gx, lax.rem(gy + gyn - 1, gyn))
    barrier = pltpu.get_barrier_semaphore()
    for who in (left, right, up, down):
        pl.semaphore_signal(barrier, inc=1, device_id=who, device_id_type=MESH)
    hz = nz * HW
    for side, start in ((0, nx - 16), (1, 0)):
        for c in range(nc):
            block = f_ref[c, :, start : start + 16, :].reshape(nz * 16, ny)
            sx[side, c * hz : (c + 1) * hz, :] = dot(take_ref[side], block).astype(BF)
    pl.semaphore_wait(barrier, 4)
    copies = []
    for side, who in ((0, right), (1, left)):
        copies.append(
            pltpu.make_async_remote_copy(
                src_ref=sx.at[side],
                dst_ref=rx.at[side],
                send_sem=ssem.at[side],
                recv_sem=rsem.at[side],
                device_id=who,
                device_id_type=MESH,
            )
        )
        copies[-1].start()

    def pack(lo, rows):
        acc = None
        for j in range(nz // 2):
            lhs = jnp.concatenate(
                [
                    p_ref[:, 2 * j + i, lo : lo + rows, :].reshape(nc * rows, ny)
                    for i in range(2)
                ],
                axis=1,
            )
            part = dot(lhs, col_ref[j])
            acc = part if acc is None else acc + part
        for side in range(2):
            sy[side, :, lo : lo + rows, :] = (
                acc[:, side * 128 : (side + 1) * 128].astype(BF).reshape(nc, rows, 128)
            )

    for c in range(nc):
        p_ref[c, :, 16 : 16 + nx, :] = f_ref[c]
    for part in range(nx // 16):
        pack(16 + 16 * part, 16)
    for side, start in ((0, 0), (1, px - 16)):
        copies[side].wait()
        for c in range(nc):
            block = dot(give_ref[side], rx[side, c * hz : (c + 1) * hz, :])
            p_ref[c, :, start : start + 16, :] = block.astype(BF).reshape(nz, 16, ny)
    pack(0, 16)
    pack(px - 16, 16)
    copies = []
    for side, who in ((0, up), (1, down)):
        copies.append(
            pltpu.make_async_remote_copy(
                src_ref=sy.at[side],
                dst_ref=yh_ref.at[side],
                send_sem=ssem.at[2 + side],
                recv_sem=rsem.at[2 + side],
                device_id=who,
                device_id_type=MESH,
            )
        )
        copies[-1].start()
    for copy in copies:
        copy.wait()


def iota(shape, dim):
    return lax.broadcasted_iota(jnp.int32, shape, dim)


def one_hot(cond):
    return jnp.where(cond, 1.0, 0.0).astype(BF)


def tile_kernel(
    gxn,
    gyn,
    list_length,
    list_ref,
    target_ref,
    p_ref,
    yh_ref,
    w_ref,
    m_ref,
    pay_ref,
    t_ref,
    qp_ref,
    qm_ref,
    r_ref,
    c_ref,
    a_ref,
    s_ref,
    cell_ref,
    count_ref,
    used_ref,
):
    nc, nz, px, ny = p_ref.shape
    across_x, across_y = (px - 32) // TE, ny // TE
    base = (lax.axis_index("gy") * gxn + lax.axis_index("gx")) * list_length
    total = jnp.int32(0)
    for e in range(list_length):
        total = total + jnp.where(target_ref[base + e] >= 0, 1, 0).astype(jnp.int32)
    quads = SPAN // 4

    @pl.loop(0, total)
    def _(t):
        tile = list_ref[base + t]
        tz = tile // (across_x * across_y)
        lx = tile // across_y % across_x
        ly = tile % across_y
        row = iota((4 * ny, 128), 0)
        col = iota((4 * ny, 128), 1)
        w = col % 32
        spread = one_hot(
            (row // ny == col // 32) & (w < SPAN) & (row % ny == ly * TE - HW + w)
        )
        x0 = pl.multiple_of(lx * TE, TE)
        for j in range(quads):
            z0 = (tz * TE - HW + 4 * j + nz) % nz
            lhs = jnp.concatenate(
                [
                    p_ref[:, z0 + i, pl.ds(x0, 48), :].reshape(nc * 48, ny)
                    for i in range(4)
                ],
                axis=1,
            )
            t_ref[j] = dot(lhs, spread)

        @pl.when((ly == 0) | (ly == across_y - 1))
        def _():
            lhs = jnp.concatenate(
                [yh_ref[side, :, pl.ds(x0, 48), :].reshape(nc * 48, 128) for side in range(2)],
                axis=1,
            )
            lane = iota((256, 128), 0)
            out = iota((256, 128), 1)
            ww = out % 32
            for j in range(quads):
                z0 = (tz * TE - HW + 4 * j + nz) % nz
                source = (z0 + out // 32) * HW
                low = (ly == 0) & (ww < HW) & (lane == source + ww)
                high = (
                    (ly == across_y - 1)
                    & (ww >= SPAN - HW)
                    & (ww < SPAN)
                    & (lane == 128 + source + ww - (SPAN - HW))
                )
                t_ref[j] = t_ref[j] + dot(lhs, one_hot(low | high))

        for j in range(quads):
            lanes = slice(j * 128, (j + 1) * 128)
            lanes_low = slice((quads + j) * 128, (quads + j + 1) * 128)
            v = [t_ref[j, c * 48 + 12 : c * 48 + 36, :] for c in range(nc)]
            plain = [v[0], v[1], v[2], v[3], v[7], v[9]]
            for i in range(3):
                pair = jnp.concatenate(plain[2 * i : 2 * i + 2], axis=0)
                qp_ref[i * 48 : i * 48 + 48, lanes] = pair.astype(BF)
            prods = [v[0] * v[c] for c in (1, 2, 3, 4, 5, 6, 8, 7)]
            prods = prods + [v[9] * (v[1 + d] - v[4 + d]) for d in range(3)]
            for i in range(6):
                if i < 5:
                    pair = jnp.concatenate(prods[2 * i : 2 * i + 2], axis=0)
                else:
                    pair = jnp.concatenate([prods[10], jnp.zeros((8, 128), F32)], axis=0)
                rows = slice(i * 48, i * 48 + pair.shape[0])
                high = pair.astype(BF)
                qm_ref[rows, lanes] = high
                qm_ref[rows, lanes_low] = (pair - high.astype(F32)).astype(BF)
        for k in range(1, HW + 1):
            rp = dot(qp_ref[...], w_ref[k - 1, : SPAN * 32, :])
            rm = dot(qm_ref[...], w_ref[k - 1])
            scale = 1.0 / (2 * k + 1) ** 3
            for h in range(2):
                r_ref[k - 1, h, :144, :] = rp[:, h * 128 : (h + 1) * 128]
                r_ref[k - 1, h, 144:, :] = rm[:, h * 128 : (h + 1) * 128]
            for h in range(2):

                def f(q):
                    acc = None
                    for d in range(-k, k + 1):
                        start = q * SPAN + HW + d
                        part = r_ref[k - 1, h, start : start + TE, :]
                        acc = part if acc is None else acc + part
                    return acc

                inv = 1.0 / f(0)
                drag = f(5) * scale
                comps = [None] * 8
                for d in range(3):
                    ag = f(6 + d)
                    comps[d] = ag * inv - f(1 + d) * scale
                    comps[3 + d] = f(14 + d) * scale - drag * ((ag - f(9 + d)) * inv)
                comps[6] = f(12) * inv
                comps[7] = f(13) * inv - f(4) * scale
                for i in range(8):
                    at = ((k - 1) * 8 + i) * TE
                    c_ref[h, at : at + TE, :] = comps[i]
        where = pl.ds(pl.multiple_of(t * 16, 16), 16)
        for par in range(2):
            for bx in range(4):
                for h in range(2):
                    acc = None
                    for r in range(4):
                        part = c_ref[h, pl.ds(par * TE + bx * 4 + r, 16, stride=2 * TE), :]
                        acc = part if acc is None else acc + part
                    at = ((par * 4 + bx) * 2 + h) * 128
                    high = acc.astype(BF)
                    a_ref[where, at : at + 128] = high
                    a_ref[where, 2048 + at : 2048 + at + 128] = (
                        acc - high.astype(F32)
                    ).astype(BF)

    s_ref[...] = dot(a_ref[...], m_ref[...])
    cells = cell_ref.shape[0]
    cell_ref[...] = jnp.zeros(cell_ref.shape, F32)
    count_ref[...] = jnp.zeros(count_ref.shape, F32)
    for g in range(gxn):
        used_ref[g] = 0

    @pl.loop(0, total)
    def _(t):
        tile = list_ref[base + t]
        lx = tile // across_y % across_x
        ly = tile % across_y
        cell = (ly // 2) * (across_x // 2) + lx // 2
        target = target_ref[base + t]
        rank = used_ref[target]
        used_ref[target] = rank + 1
        stats = s_ref[pl.ds(pl.multiple_of(t * 16, 16), 16), :]
        pay_ref[target, pl.ds(pl.multiple_of(rank * 16, 16), 16), :] = stats
        cell_ref[cell] = cell_ref[cell] + stats
        count_ref[cell] = count_ref[cell] + 1.0

    lane = iota((16, 128), 1)
    row = iota((16, 128), 0)
    rows = []
    for cell in range(cells):
        sums = cell_ref[cell]
        even = jnp.sum(jnp.where(lane < 64, sums, 0.0), axis=1, keepdims=True)
        odd = jnp.sum(jnp.where(lane >= 64, sums, 0.0), axis=1, keepdims=True)
        spot = lane % 32
        placed = jnp.where(spot == 2 * row, even, jnp.where(spot == 2 * row + 1, odd, 0.0))
        sums = jnp.sum(placed, axis=0, keepdims=True) * (1.0 / 64.0)
        rows.append(sums / jnp.maximum(count_ref[cell, 0:1, :], 1.0))
    coarse = jnp.concatenate(rows, axis=0)
    for g in range(gxn):
        pay_ref[g, CAP * 16 : CAP * 16 + cells, :] = coarse


def exchange_kernel(gxn, gyn, pay_ref, got_ref, all_ref, mine, xs, xr, ys, yr):
    gx, gy = lax.axis_index("gx"), lax.axis_index("gy")
    barrier = pltpu.get_barrier_semaphore()
    for d in range(1, gxn):
        pl.semaphore_signal(
            barrier, inc=1, device_id=(lax.rem(gx + d, gxn), gy), device_id_type=MESH
        )
    for d in range(1, gyn):
        pl.semaphore_signal(
            barrier, inc=1, device_id=(gx, lax.rem(gy + d, gyn)), device_id_type=MESH
        )
    pl.semaphore_wait(barrier, gxn + gyn - 2)
    copies = []
    for d in range(1, gxn):
        who = lax.rem(gx + d, gxn)
        copies.append(
            pltpu.make_async_remote_copy(
                src_ref=pay_ref.at[who],
                dst_ref=got_ref.at[gx],
                send_sem=xs.at[d],
                recv_sem=xr.at[d],
                device_id=(who, gy),
                device_id_type=MESH,
            )
        )
        copies[-1].start()
    got_ref[gx] = pay_ref[gx]
    for copy in copies:
        copy.wait()
    cells = mine.shape[1]
    for g in range(gxn):
        mine[g] = got_ref[g, CAP * 16 : CAP * 16 + cells, :]
    copies = []
    for d in range(1, gyn):
        copies.append(
            pltpu.make_async_remote_copy(
                src_ref=mine,
                dst_ref=all_ref.at[gy],
                send_sem=ys.at[d],
                recv_sem=yr.at[d],
                device_id=(gx, lax.rem(gy + d, gyn)),
                device_id_type=MESH,
            )
        )
        copies[-1].start()
    all_ref[gy] = mine[...]
    for copy in copies:
        copy.wait()


def select_kernel(
    gxn, gyn, list_length, cells_x, target_ref, order_ref, got_ref, all_ref, o_ref, c_ref
):
    gx, gy = lax.axis_index("gx"), lax.axis_index("gy")

    def source(s, slot):
        def entry(e, carry):
            slot, rank = carry
            hit = target_ref[(gy * gxn + s) * list_length + e] == gx

            @pl.when(hit)
            def _():
                at = pl.multiple_of(rank * 16, 16)
                o_ref[slot] = got_ref[s, pl.ds(at, 16), :]

            step = jnp.where(hit, 1, 0).astype(jnp.int32)
            return slot + step, rank + step

        return lax.fori_loop(0, list_length, entry, (slot, jnp.int32(0)))[0]

    lax.fori_loop(0, gxn, source, jnp.int32(0))
    per_row = c_ref.shape[0]
    cells_y = all_ref.shape[2] // cells_x
    group = iota((1, 128), 1) // 32
    for r in range(per_row):
        pencil = order_ref[gy * per_row + r]
        owner = pencil // cells_y
        first = pencil % cells_y * cells_x
        for part in range(c_ref.shape[1] // 128):
            row = None
            for i in range(4):
                cx = part * 4 + i
                value = all_ref[owner, cx // cells_x, pl.ds(first + cx % cells_x, 1), :]
                row = value if row is None else jnp.where(group == i, value, row)
            c_ref[r : r + 1, part * 128 : (part + 1) * 128] = row


VM = pl.BlockSpec(memory_space=pltpu.VMEM)
SM = pl.BlockSpec(memory_space=pltpu.SMEM)


def shards(gxn, gyn, fields, dense_list, filter_device, pencil_order):
    nc, nz, nx, ny = fields.shape
    list_length = dense_list.shape[2]
    per_filter = gxn // 4 * (CAP + (CAP - 1) // 2)
    cells_x = nx // TE // 2
    cells = cells_x * (ny // TE // 2)
    pencils = pencil_order.shape[0]
    px = nx + 32
    take, give = edge_weights(nz)
    padded, columns = pl.pallas_call(
        functools.partial(halo_kernel, gxn, gyn),
        out_shape=(
            jax.ShapeDtypeStruct((nc, nz, px, ny), BF),
            jax.ShapeDtypeStruct((2, nc, px, 128), BF),
        ),
        in_specs=[VM] * 4,
        out_specs=(VM, VM),
        scratch_shapes=[
            pltpu.VMEM((2, nc * nz * HW, ny), BF),
            pltpu.VMEM((2, nc * nz * HW, ny), BF),
            pltpu.VMEM((2, nc, px, 128), BF),
            pltpu.SemaphoreType.DMA((4,)),
            pltpu.SemaphoreType.DMA((4,)),
        ],
        compiler_params=pltpu.CompilerParams(
            collective_id=0, has_side_effects=True, vmem_limit_bytes=40 << 20
        ),
        name="halo",
    )(fields, jnp.asarray(take), jnp.asarray(give), jnp.asarray(column_weights(nz, ny)))
    lists = dense_list.reshape(-1)
    targets = filter_device.reshape(-1)
    payload = pl.pallas_call(
        functools.partial(tile_kernel, gxn, gyn, list_length),
        out_shape=jax.ShapeDtypeStruct((gxn, CAP * 16 + cells, 128), F32),
        in_specs=[SM, SM, VM, VM, VM, VM],
        out_specs=VM,
        scratch_shapes=[
            pltpu.VMEM((SPAN // 4, nc * 48, 128), F32),
            pltpu.VMEM((144, SPAN * 32), BF),
            pltpu.VMEM((272, 2 * SPAN * 32), BF),
            pltpu.VMEM((HW, 2, 416, 128), F32),
            pltpu.VMEM((2, HW * 8 * TE, 128), F32),
            pltpu.VMEM((list_length * 16, 4096), BF),
            pltpu.VMEM((list_length * 16, 128), F32),
            pltpu.VMEM((cells, 16, 128), F32),
            pltpu.VMEM((cells, 8, 128), F32),
            pltpu.SMEM((gxn,), jnp.int32),
        ],
        compiler_params=pltpu.CompilerParams(vmem_limit_bytes=40 << 20),
        name="tiles",
    )(
        lists,
        targets,
        padded,
        columns,
        jnp.asarray(window_weights()),
        jnp.asarray(block_weights()),
    )
    got, every = pl.pallas_call(
        functools.partial(exchange_kernel, gxn, gyn),
        out_shape=(
            jax.ShapeDtypeStruct(payload.shape, F32),
            jax.ShapeDtypeStruct((gyn, gxn, cells, 128), F32),
        ),
        in_specs=[VM],
        out_specs=(VM, VM),
        scratch_shapes=[
            pltpu.VMEM((gxn, cells, 128), F32),
            pltpu.SemaphoreType.DMA((gxn,)),
            pltpu.SemaphoreType.DMA((gxn,)),
            pltpu.SemaphoreType.DMA((gyn,)),
            pltpu.SemaphoreType.DMA((gyn,)),
        ],
        compiler_params=pltpu.CompilerParams(collective_id=1, has_side_effects=True),
        name="exchange",
    )(payload)
    statistics, coarse = pl.pallas_call(
        functools.partial(select_kernel, gxn, gyn, list_length, cells_x),
        out_shape=(
            jax.ShapeDtypeStruct((per_filter, 16, 128), F32),
            jax.ShapeDtypeStruct((pencils // gyn, cells_x * gxn * HW * 8), F32),
        ),
        in_specs=[SM, SM, VM, VM],
        out_specs=(VM, VM),
        name="select",
    )(targets, pencil_order, got, every)
    return statistics.reshape(per_filter, 2048), coarse


def solution(mesh):
    in_specs = (P(None, None, "gx", "gy"), P(), P(), P())
    out_specs = (P(("gx", "gy"), None), P("gy", None))
    body = functools.partial(shards, mesh.shape["gx"], mesh.shape["gy"])
    return jax.shard_map(
        body, mesh=mesh, in_specs=in_specs, out_specs=out_specs, check_vma=False
    )
```

profile of v0, /device:TPU:0, one launch (start us, length us, event | category | flops | bytes accessed | tf_op | source)
XLA Modules:
  0.0 91.3 jit_solution(14882326647721158939)
XLA Ops:
  0.6 0.8 reshape.13.target_ref
  1.4 0.0 copy-start.8
  1.5 0.8 reshape.14.list_ref
  2.3 0.0 copy-start.1
  2.3 2.5 %copy-done.1 = bf16[10,32,64,128]{3,2,1,0:T(8,128)(2,1)S(1)} copy-done((bf16[10,32,64,128]{3,2,1,0:T(8,128)(2,1)S(1)}, bf16[10,32,64,128]{3,2,1,0:T(8,128)(2,1)}, u32[]{:S(2)}) %copy-start.1) | copy-done | bytes 5242904
  4.8 0.0 copy-start.3
  4.8 1.6 %copy-done.3 = bf16[16,256,256]{2,1,0:T(8,128)(2,1)S(1)} copy-done((bf16[16,256,256]{2,1,0:T(8,128)(2,1)S(1)}, bf16[16,256,256]{2,1,0:T(8,128)(2,1)}, u32[]{:S(2)}) %copy-start.3) | copy-done | bytes 2097176
  6.4 0.9 %copy-done.6 = bf16[2,512,128]{2,1,0:T(8,128)(2,1)S(1)} copy-done((bf16[2,512,128]{2,1,0:T(8,128)(2,1)S(1)}, bf16[2,512,128]{2,1,0:T(8,128)(2,1)}, u32[]{:S(2)}) %copy-start.6) | copy-done | bytes 262168
  7.3 0.0 copy-start.7
  7.3 0.9 %copy-done.7 = bf16[2,128,512]{2,1,0:T(8,128)(2,1)S(1)} copy-done((bf16[2,128,512]{2,1,0:T(8,128)(2,1)S(1)}, bf16[2,128,512]{2,1,0:T(8,128)(2,1)}, u32[]{:S(2)}) %copy-start.7) | copy-done | bytes 262168
  8.3 0.0 copy-start.2
  8.3 0.0 copy-start.4
  8.3 29.5 %halo.1 = (bf16[10,32,96,128]{3,2,1,0:T(8,128)(2,1)}, bf16[2,10,96,128]{3,2,1,0:T(8,128)(2,1)S(1)}) custom-call(bf16[10,32,64,128]{3,2,1,0:T(8,128)(2,1)S(1)} %copy-done.1, bf16[2,128,512]{2,1,0:T(8,128)(2,1)S(1)} %copy-done.7, bf16[2,512,128]{2,1,0:T(8,128)(2,1)S(1)} %copy-done.6, bf16[16,256,256]{2,1,0:T(8,128)(2,1)S(1)} %copy-done.3), custom_call_target="tpu_custom_call" | custom-call | tf_op jit(solution)/shard_map/halo/pallas_call | solution.py:432
  37.8 0.0 copy-done.2
  37.8 0.0 copy-done.4
  37.8 0.0 copy-start
  37.8 3.2 %copy-done = bf16[10,32,96,128]{3,2,1,0:T(8,128)(2,1)S(1)} copy-done((bf16[10,32,96,128]{3,2,1,0:T(8,128)(2,1)S(1)}, bf16[10,32,96,128]{3,2,1,0:T(8,128)(2,1)}, u32[]{:S(2)}) %copy-start) | copy-done | bytes 7864344
  41.0 32.4 %tiles.1.pay_ref = f32[8,40,128]{2,1,0:T(8,128)S(1)} custom-call(s32[320]{0:T(512)S(1)} %reshape.14.list_ref, s32[320]{0:T(512)S(1)} %reshape.13.target_ref, bf16[10,32,96,128]{3,2,1,0:T(8,128)(2,1)S(1)} %copy-done, bf16[2,10,96,128]{3,2,1,0:T(8,128)(2,1)S(1)} %get-tuple-element.9.yh_ref, bf16[4,1536,256]{2,1,0:T(8,128)(2,1)S(1)} %copy-done.2, ...), custom_call_target="tpu_custom_call" | custom-call | tf_op jit(solution)/shard_map/tiles/pallas_call | solution.py:454
  73.4 0.0 copy-done.8
  73.4 0.0 copy-start.5
  73.4 0.7 copy-done.5
  74.1 12.8 %exchange.1 = (f32[8,40,128]{2,1,0:T(8,128)}, f32[4,8,8,128]{3,2,1,0:T(8,128)}) custom-call(f32[8,40,128]{2,1,0:T(8,128)} %copy-done.5), custom_call_target="tpu_custom_call" | custom-call | tf_op jit(solution)/shard_map/exchange/pallas_call | solution.py:481
  86.9 3.1 %select.1 = (f32[4,16,128]{2,1,0:T(8,128)}, f32[4,512]{1,0:T(4,128)}) custom-call(s32[320]{0:T(512)} %copy-done.8, s32[16]{0:T(128)} %order_ref.1, f32[8,40,128]{2,1,0:T(8,128)} %get-tuple-element.10.got_ref, f32[4,8,8,128]{3,2,1,0:T(8,128)} %get-tuple-element.11.all_ref), custom_call_target="tpu_custom_call" | custom-call | tf_op jit(solution)/shard_map/select/pallas_call | solution.py:499
  89.9 1.4 %copy.13 = f32[1,4,16,128]{3,1,2,0:T(4,128)} copy(f32[1,4,16,128]{3,2,1,0:T(8,128)} %bitcast.5) | data formatting | bytes 65536
  (1 shorter events, 0.0 us)
Async XLA Ops:
  1.4 72.0 %copy-start.8 = (s32[320]{0:T(512)}, s32[320]{0:T(512)S(1)}, u32[]{:S(2)}) copy-start(s32[320]{0:T(512)S(1)} %reshape.13.target_ref) | copy-start | bytes 3844
  2.3 2.5 %copy-start.1 = (bf16[10,32,64,128]{3,2,1,0:T(8,128)(2,1)S(1)}, bf16[10,32,64,128]{3,2,1,0:T(8,128)(2,1)}, u32[]{:S(2)}) copy-start(bf16[10,32,64,128]{3,2,1,0:T(8,128)(2,1)} %f_ref.1) | copy-start | bytes 15728644
  4.8 1.6 %copy-start.3 = (bf16[16,256,256]{2,1,0:T(8,128)(2,1)S(1)}, bf16[16,256,256]{2,1,0:T(8,128)(2,1)}, u32[]{:S(2)}) copy-start(bf16[16,256,256]{2,1,0:T(8,128)(2,1)} %constant.12.clone.col_ref) | copy-start | bytes 6291460
  6.4 0.9 %copy-start.6 = (bf16[2,512,128]{2,1,0:T(8,128)(2,1)S(1)}, bf16[2,512,128]{2,1,0:T(8,128)(2,1)}, u32[]{:S(2)}) copy-start(bf16[2,512,128]{2,1,0:T(8,128)(2,1)} %constant.11.clone.give_ref) | copy-start | bytes 786436
  7.3 0.9 %copy-start.7 = (bf16[2,128,512]{2,1,0:T(8,128)(2,1)S(1)}, bf16[2,128,512]{2,1,0:T(8,128)(2,1)}, u32[]{:S(2)}) copy-start(bf16[2,128,512]{2,1,0:T(8,128)(2,1)} %constant.10.clone.take_ref) | copy-start | bytes 786436
  8.3 29.5 %copy-start.2 = (bf16[4,1536,256]{2,1,0:T(8,128)(2,1)S(1)}, bf16[4,1536,256]{2,1,0:T(8,128)(2,1)}, u32[]{:S(2)}) copy-start(bf16[4,1536,256]{2,1,0:T(8,128)(2,1)} %constant.13.clone.w_ref) | copy-start | bytes 9437188
  8.3 29.5 %copy-start.4 = (bf16[4096,128]{1,0:T(8,128)(2,1)S(1)}, bf16[4096,128]{1,0:T(8,128)(2,1)}, u32[]{:S(2)}) copy-start(bf16[4096,128]{1,0:T(8,128)(2,1)} %constant.14.clone.m_ref) | copy-start | bytes 3145732
  37.8 3.2 %copy-start = (bf16[10,32,96,128]{3,2,1,0:T(8,128)(2,1)S(1)}, bf16[10,32,96,128]{3,2,1,0:T(8,128)(2,1)}, u32[]{:S(2)}) copy-start(bf16[10,32,96,128]{3,2,1,0:T(8,128)(2,1)} %get-tuple-element.8.p_ref) | copy-start | bytes 23592964
  73.4 0.7 copy-start.5
where the time goes:
time: 91.7 us; the launch traced here: 91.3 us
  Pallas kernels  77.7 us (85%)
  local copies, waits for them, and re-layouts  12.9 us (14%)
    pallas_call x1, Pallas kernels, shards(): pl.pallas_call(functools.partial(tile_kernel, gxn, gyn, list_length), out...  32.4 us
    pallas_call x1, Pallas kernels, shards(): pl.pallas_call(functools.partial(halo_kernel, gxn, gyn), out_shape=(jax.S...  29.5 us
    pallas_call x1, Pallas kernels, shards(): pl.pallas_call(functools.partial(exchange_kernel, gxn, gyn), out_shape=(j...  12.8 us
    unnamed x19, local copies, waits for them, and re-layouts  11.3 us
    pallas_call x1, Pallas kernels, shards(): pl.pallas_call(functools.partial(select_kernel, gxn, gyn, list_length, ce...  3.09 us

commit v1 on v0

--- a/solution.py
+++ b/solution.py
@@ -46,33 +46,8 @@
     return np.concatenate([m, m], axis=0).astype(jnp.bfloat16)
 
 
-def edge_weights(nz):
-    z = np.arange(nz)[:, None, None, None]
-    r = np.arange(HW)[None, :, None, None]
-    zs = np.arange(nz)[None, None, :, None]
-    s = np.arange(16)[None, None, None, :]
-    last = ((z == zs) & (s == 12 + r)).reshape(nz * HW, nz * 16)
-    first = ((z == zs) & (s == r)).reshape(nz * HW, nz * 16)
-    take = np.stack([last, first])
-    give = np.stack([last.T, first.T])
-    return take.astype(jnp.bfloat16), give.astype(jnp.bfloat16)
-
-
-def column_weights(nz, ny):
-    z = np.arange(nz)[:, None, None, None]
-    y = np.arange(ny)[None, :, None, None]
-    side = np.arange(2)[None, None, :, None]
-    lane = np.arange(128)[None, None, None, :]
-    low = (side == 0) & (y >= ny - HW) & (lane == z * HW + y - (ny - HW))
-    high = (side == 1) & (y < HW) & (lane == z * HW + y)
-    return (low | high).reshape(nz // 2, 2 * ny, 256).astype(jnp.bfloat16)
-
-
-def halo_kernel(
-    gxn, gyn, f_ref, take_ref, give_ref, col_ref, p_ref, yh_ref, sx, rx, sy, ssem, rsem
-):
+def halo_kernel(gxn, gyn, f_ref, e_ref, yh_ref, yc_ref, col, sx, rx, sy, sc, ssem, rsem):
     nc, nz, nx, ny = f_ref.shape
-    px = nx + 32
     gx, gy = lax.axis_index("gx"), lax.axis_index("gy")
     right = (lax.rem(gx + 1, gxn), gy)
     left = (lax.rem(gx + gxn - 1, gxn), gy)
@@ -82,67 +57,78 @@
     for who in (left, right, up, down):
         pl.semaphore_signal(barrier, inc=1, device_id=who, device_id_type=MESH)
     hz = nz * HW
-    for side, start in ((0, nx - 16), (1, 0)):
-        for c in range(nc):
-            block = f_ref[c, :, start : start + 16, :].reshape(nz * 16, ny)
-            sx[side, c * hz : (c + 1) * hz, :] = dot(take_ref[side], block).astype(BF)
-    pl.semaphore_wait(barrier, 4)
-    copies = []
-    for side, who in ((0, right), (1, left)):
-        copies.append(
-            pltpu.make_async_remote_copy(
-                src_ref=sx.at[side],
-                dst_ref=rx.at[side],
-                send_sem=ssem.at[side],
-                recv_sem=rsem.at[side],
-                device_id=who,
-                device_id_type=MESH,
-            )
+
+    def send(src, dst, sem, who):
+        copy = pltpu.make_async_remote_copy(
+            src_ref=src,
+            dst_ref=dst,
+            send_sem=ssem.at[sem],
+            recv_sem=rsem.at[sem],
+            device_id=who,
+            device_id_type=MESH,
         )
-        copies[-1].start()
-
-    def pack(lo, rows):
+        copy.start()
+        return copy
+
+    row = iota((2 * ny, 256), 0)
+    lane = iota((2 * ny, 256), 1)
+    y, l = row % ny, lane % 128
+    spot = l - row // ny * HW
+    low = jnp.where((lane < 128) & (y >= ny - HW), spot - y + (ny - HW), -1)
+    base = jnp.where((lane >= 128) & (y < HW), spot - y, low)
+    for j in range(nz // 2):
+        col[j] = one_hot(base == 2 * HW * j)
+
+    def pack(ref, lo):
         acc = None
         for j in range(nz // 2):
             lhs = jnp.concatenate(
-                [
-                    p_ref[:, 2 * j + i, lo : lo + rows, :].reshape(nc * rows, ny)
-                    for i in range(2)
-                ],
+                [ref[:, 2 * j + i, lo : lo + 16, :].reshape(nc * 16, ny) for i in range(2)],
                 axis=1,
             )
-            part = dot(lhs, col_ref[j])
+            part = dot(lhs, col[j])
             acc = part if acc is None else acc + part
+        return [
+            acc[:, side * 128 : (side + 1) * 128].astype(BF).reshape(nc, 16, 128)
+            for side in range(2)
+        ]
+
+    out = iota((hz, nz * 16), 0)
+    put = iota((hz, nz * 16), 1)
+    same = out // HW == put // 16
+    pl.semaphore_wait(barrier, 4)
+    xcopies = []
+    for side, start, first, who in ((0, nx - 16, 16 - HW, right), (1, 0, 0, left)):
+        take = one_hot(same & (put % 16 == first + out % HW))
+        for c in range(nc):
+            block = f_ref[c, :, start : start + 16, :].reshape(nz * 16, ny)
+            sx[side, c * hz : (c + 1) * hz, :] = dot(take, block).astype(BF)
+        xcopies.append(send(sx.at[side], rx.at[side], side, who))
+    for part in range(nx // 16):
+        both = pack(f_ref, part * 16)
         for side in range(2):
-            sy[side, :, lo : lo + rows, :] = (
-                acc[:, side * 128 : (side + 1) * 128].astype(BF).reshape(nc, rows, 128)
-            )
-
+            sy[side, :, part * 16 : part * 16 + 16, :] = both[side]
+    ycopies = [send(sy.at[0], yh_ref.at[0], 2, up), send(sy.at[1], yh_ref.at[1], 3, down)]
+    put = iota((nz * 16, 2 * hz), 0)
+    src = iota((nz * 16, 2 * hz), 1)
+    code = put - put // 16 * 16
+    inner = src % hz
+    give = one_hot(
+        (put // 16 == inner // HW)
+        & (code == inner % HW + jnp.where(src < hz, 16 - HW, 0))
+    )
+    for copy in xcopies:
+        copy.wait()
     for c in range(nc):
-        p_ref[c, :, 16 : 16 + nx, :] = f_ref[c]
-    for part in range(nx // 16):
-        pack(16 + 16 * part, 16)
-    for side, start in ((0, 0), (1, px - 16)):
-        copies[side].wait()
-        for c in range(nc):
-            block = dot(give_ref[side], rx[side, c * hz : (c + 1) * hz, :])
-            p_ref[c, :, start : start + 16, :] = block.astype(BF).reshape(nz, 16, ny)
-    pack(0, 16)
-    pack(px - 16, 16)
-    copies = []
-    for side, who in ((0, up), (1, down)):
-        copies.append(
-            pltpu.make_async_remote_copy(
-                src_ref=sy.at[side],
-                dst_ref=yh_ref.at[side],
-                send_sem=ssem.at[2 + side],
-                recv_sem=rsem.at[2 + side],
-                device_id=who,
-                device_id_type=MESH,
-            )
-        )
-        copies[-1].start()
-    for copy in copies:
+        rows = slice(c * hz, (c + 1) * hz)
+        block = dot(give, jnp.concatenate([rx[0, rows, :], rx[1, rows, :]], axis=0))
+        e_ref[c] = block.astype(BF).reshape(nz, 16, ny)
+    both = pack(e_ref, 0)
+    for side in range(2):
+        sc[side] = both[side]
+    ycopies.append(send(sc.at[0], yc_ref.at[0], 4, up))
+    ycopies.append(send(sc.at[1], yc_ref.at[1], 5, down))
+    for copy in ycopies:
         copy.wait()
 
 
@@ -160,8 +146,10 @@
     list_length,
     list_ref,
     target_ref,
-    p_ref,
+    f_ref,
+    e_ref,
     yh_ref,
+    yc_ref,
     w_ref,
     m_ref,
     pay_ref,
@@ -176,17 +164,17 @@
     count_ref,
     used_ref,
 ):
-    nc, nz, px, ny = p_ref.shape
-    across_x, across_y = (px - 32) // TE, ny // TE
-    base = (lax.axis_index("gy") * gxn + lax.axis_index("gx")) * list_length
+    nc, nz, nx, ny = f_ref.shape
+    across_x, across_y = nx // TE, ny // TE
+    gx, gy = lax.axis_index("gx"), lax.axis_index("gy")
     total = jnp.int32(0)
     for e in range(list_length):
-        total = total + jnp.where(target_ref[base + e] >= 0, 1, 0).astype(jnp.int32)
+        total = total + jnp.where(target_ref[gy, gx, e] >= 0, 1, 0).astype(jnp.int32)
     quads = SPAN // 4
 
     @pl.loop(0, total)
     def _(t):
-        tile = list_ref[base + t]
+        tile = list_ref[gy, gx, t]
         tz = tile // (across_x * across_y)
         lx = tile // across_y % across_x
         ly = tile % across_y
@@ -197,11 +185,19 @@
             (row // ny == col // 32) & (w < SPAN) & (row % ny == ly * TE - HW + w)
         )
         x0 = pl.multiple_of(lx * TE, TE)
+        x_low = pl.multiple_of(jnp.maximum(lx - 1, 0) * TE, TE)
+        x_high = pl.multiple_of(jnp.minimum(lx + 1, across_x - 1) * TE, TE)
+
+        def three(own, edge):
+            low = jnp.where(lx == 0, edge, own(x_low))
+            high = jnp.where(lx == across_x - 1, edge, own(x_high))
+            return jnp.concatenate([low, own(x0), high], axis=1).reshape(nc * 48, 128)
+
         for j in range(quads):
             z0 = (tz * TE - HW + 4 * j + nz) % nz
             lhs = jnp.concatenate(
                 [
-                    p_ref[:, z0 + i, pl.ds(x0, 48), :].reshape(nc * 48, ny)
+                    three(lambda x, i=i: f_ref[:, z0 + i, pl.ds(x, 16), :], e_ref[:, z0 + i])
                     for i in range(4)
                 ],
                 axis=1,
@@ -211,7 +207,7 @@
         @pl.when((ly == 0) | (ly == across_y - 1))
         def _():
             lhs = jnp.concatenate(
-                [yh_ref[side, :, pl.ds(x0, 48), :].reshape(nc * 48, 128) for side in range(2)],
+                [three(lambda x, i=i: yh_ref[i, :, pl.ds(x, 16), :], yc_ref[i]) for i in range(2)],
                 axis=1,
             )
             lane = iota((256, 128), 0)
@@ -301,11 +297,11 @@
 
     @pl.loop(0, total)
     def _(t):
-        tile = list_ref[base + t]
+        tile = list_ref[gy, gx, t]
         lx = tile // across_y % across_x
         ly = tile % across_y
         cell = (ly // 2) * (across_x // 2) + lx // 2
-        target = target_ref[base + t]
+        target = target_ref[gy, gx, t]
         rank = used_ref[target]
         used_ref[target] = rank + 1
         stats = s_ref[pl.ds(pl.multiple_of(t * 16, 16), 16), :]
@@ -380,19 +376,19 @@
 
 
 def select_kernel(
-    gxn, gyn, list_length, cells_x, target_ref, order_ref, got_ref, all_ref, o_ref, c_ref
+    gxn, gyn, list_length, cells_x, target_ref, order_ref, got_ref, all_ref, o_ref, c_ref, held
 ):
     gx, gy = lax.axis_index("gx"), lax.axis_index("gy")
 
     def source(s, slot):
         def entry(e, carry):
             slot, rank = carry
-            hit = target_ref[(gy * gxn + s) * list_length + e] == gx
+            hit = target_ref[gy, s, e] == gx
 
             @pl.when(hit)
             def _():
                 at = pl.multiple_of(rank * 16, 16)
-                o_ref[slot] = got_ref[s, pl.ds(at, 16), :]
+                held[slot] = got_ref[s, pl.ds(at, 16), :]
 
             step = jnp.where(hit, 1, 0).astype(jnp.int32)
             return slot + step, rank + step
@@ -400,6 +396,9 @@
         return lax.fori_loop(0, list_length, entry, (slot, jnp.int32(0)))[0]
 
     lax.fori_loop(0, gxn, source, jnp.int32(0))
+    for slot in range(o_ref.shape[0]):
+        for r in range(16):
+            o_ref[slot : slot + 1, r * 128 : (r + 1) * 128] = held[slot, r : r + 1, :]
     per_row = c_ref.shape[0]
     cells_y = all_ref.shape[2] // cells_x
     group = iota((1, 128), 1) // 32
@@ -427,34 +426,33 @@
     cells_x = nx // TE // 2
     cells = cells_x * (ny // TE // 2)
     pencils = pencil_order.shape[0]
-    px = nx + 32
-    take, give = edge_weights(nz)
-    padded, columns = pl.pallas_call(
+    edges, columns, corners = pl.pallas_call(
         functools.partial(halo_kernel, gxn, gyn),
         out_shape=(
-            jax.ShapeDtypeStruct((nc, nz, px, ny), BF),
-            jax.ShapeDtypeStruct((2, nc, px, 128), BF),
+            jax.ShapeDtypeStruct((nc, nz, 16, ny), BF),
+            jax.ShapeDtypeStruct((2, nc, nx, 128), BF),
+            jax.ShapeDtypeStruct((2, nc, 16, 128), BF),
         ),
-        in_specs=[VM] * 4,
-        out_specs=(VM, VM),
+        in_specs=[VM],
+        out_specs=(VM, VM, VM),
         scratch_shapes=[
+            pltpu.VMEM((nz // 2, 2 * ny, 256), BF),
             pltpu.VMEM((2, nc * nz * HW, ny), BF),
             pltpu.VMEM((2, nc * nz * HW, ny), BF),
-            pltpu.VMEM((2, nc, px, 128), BF),
-            pltpu.SemaphoreType.DMA((4,)),
-            pltpu.SemaphoreType.DMA((4,)),
+            pltpu.VMEM((2, nc, nx, 128), BF),
+            pltpu.VMEM((2, nc, 16, 128), BF),
+            pltpu.SemaphoreType.DMA((6,)),
+            pltpu.SemaphoreType.DMA((6,)),
         ],
         compiler_params=pltpu.CompilerParams(
             collective_id=0, has_side_effects=True, vmem_limit_bytes=40 << 20
         ),
         name="halo",
-    )(fields, jnp.asarray(take), jnp.asarray(give), jnp.asarray(column_weights(nz, ny)))
-    lists = dense_list.reshape(-1)
-    targets = filter_device.reshape(-1)
+    )(fields)
     payload = pl.pallas_call(
         functools.partial(tile_kernel, gxn, gyn, list_length),
         out_shape=jax.ShapeDtypeStruct((gxn, CAP * 16 + cells, 128), F32),
-        in_specs=[SM, SM, VM, VM, VM, VM],
+        in_specs=[SM, SM] + [VM] * 6,
         out_specs=VM,
         scratch_shapes=[
             pltpu.VMEM((SPAN // 4, nc * 48, 128), F32),
@@ -471,10 +469,12 @@
         compiler_params=pltpu.CompilerParams(vmem_limit_bytes=40 << 20),
         name="tiles",
     )(
-        lists,
-        targets,
-        padded,
+        dense_list,
+        filter_device,
+        fields,
+        edges,
         columns,
+        corners,
         jnp.asarray(window_weights()),
         jnp.asarray(block_weights()),
     )
@@ -499,14 +499,15 @@
     statistics, coarse = pl.pallas_call(
         functools.partial(select_kernel, gxn, gyn, list_length, cells_x),
         out_shape=(
-            jax.ShapeDtypeStruct((per_filter, 16, 128), F32),
+            jax.ShapeDtypeStruct((per_filter, 2048), F32),
             jax.ShapeDtypeStruct((pencils // gyn, cells_x * gxn * HW * 8), F32),
         ),
         in_specs=[SM, SM, VM, VM],
         out_specs=(VM, VM),
+        scratch_shapes=[pltpu.VMEM((per_filter, 16, 128), F32)],
         name="select",
-    )(targets, pencil_order, got, every)
-    return statistics.reshape(per_filter, 2048), coarse
+    )(filter_device, pencil_order, got, every)
+    return statistics, coarse
 
 
 def solution(mesh):

time: 91.7 us -> 71.4 us (0.78)
  Pallas kernels: 77.7 us -> 67.5 us
  local copies, waits for them, and re-layouts: 12.9 us -> 3.14 us
    pallas_call x1, Pallas kernels: 29.5 us -> 19.4 us  [shards(): pl.pallas_call(functools.partial(halo_kernel, gxn, gyn), out_shape=(jax.S...]
    unnamed x19 -> x12, local copies, waits for them, and re-layouts: 11.3 us -> 3.14 us
    reshape x2 -> x0, local copies, waits for them, and re-layouts: 1.64 us -> none  [the longest x1 0.82 us: shards(): lists = dense_list.reshape(-1)]
where the time goes in v1:
time: 71.4 us; the launch traced here: 71.3 us
  Pallas kernels  67.5 us (95%)
  local copies, waits for them, and re-layouts  3.14 us (4%)
    pallas_call x1, Pallas kernels, shards(): pl.pallas_call(functools.partial(tile_kernel, gxn, gyn, list_length), out...  31.7 us
    pallas_call x1, Pallas kernels, shards(): pl.pallas_call(functools.partial(halo_kernel, gxn, gyn), out_shape=(jax.S...  19.4 us
    pallas_call x1, Pallas kernels, shards(): pl.pallas_call(functools.partial(exchange_kernel, gxn, gyn), out_shape=(j...  13.3 us
    unnamed x12, local copies, waits for them, and re-layouts  3.14 us
    pallas_call x1, Pallas kernels, shards(): pl.pallas_call(functools.partial(select_kernel, gxn, gyn, list_length, ce...  3.11 us

profile of v1, /device:TPU:0, one launch (start us, length us, event | category | flops | bytes accessed | tf_op | source)
XLA Modules:
  0.0 71.3 jit_solution(9864282242917506519)
XLA Ops:
  0.6 0.0 copy-start
  0.6 2.5 %copy-done = bf16[10,32,64,128]{3,2,1,0:T(8,128)(2,1)S(1)} copy-done((bf16[10,32,64,128]{3,2,1,0:T(8,128)(2,1)S(1)}, bf16[10,32,64,128]{3,2,1,0:T(8,128)(2,1)}, u32[]{:S(2)}) %copy-start) | copy-done | bytes 5242904
  3.1 0.0 copy-start.1
  3.1 0.0 copy-start.2
  3.1 0.0 copy-start.4
  3.1 0.0 copy-start.5
  3.1 19.4 %halo.1 = (bf16[10,32,16,128]{3,2,1,0:T(8,128)(2,1)S(1)}, bf16[2,10,64,128]{3,2,1,0:T(8,128)(2,1)S(1)}, bf16[2,10,16,128]{3,2,1,0:T(8,128)(2,1)S(1)}) custom-call(bf16[10,32,64,128]{3,2,1,0:T(8,128)(2,1)S(1)} %copy-done), custom_call_target="tpu_custom_call" | custom-call | tf_op jit(solution)/shard_map/halo/pallas_call | solution.py:429
  22.5 0.0 copy-done.1
  22.5 0.0 copy-done.2
  22.5 0.0 copy-done.4
  22.5 0.0 copy-done.5
  22.5 31.7 %tiles.1.pay_ref = f32[8,40,128]{2,1,0:T(8,128)S(1)} custom-call(s32[4,8,10]{2,1,0:T(8,128)S(1)} %copy-done.5, s32[4,8,10]{2,1,0:T(8,128)S(1)} %copy-done.4, bf16[10,32,64,128]{3,2,1,0:T(8,128)(2,1)S(1)} %copy-done, bf16[10,32,16,128]{3,2,1,0:T(8,128)(2,1)S(1)} %get-tuple-element.7.e_ref, bf16[2,10,64,128]{3,2,1,0:T(8,128)(2,1)S(1)} %get-tuple-element.8.yh_ref, ...), custom_call_target="tpu_custom_call" | custom-call | tf_op jit(solution)/shard_map/tiles/pallas_call | solution.py:452
  54.2 0.0 copy-start.3
  54.3 0.6 copy-done.3
  54.9 13.3 %exchange.1 = (f32[8,40,128]{2,1,0:T(8,128)}, f32[4,8,8,128]{3,2,1,0:T(8,128)}) custom-call(f32[8,40,128]{2,1,0:T(8,128)} %copy-done.3), custom_call_target="tpu_custom_call" | custom-call | tf_op jit(solution)/shard_map/exchange/pallas_call | solution.py:481
  68.2 3.1 %select.1 = (f32[4,2048]{1,0:T(4,128)}, f32[4,512]{1,0:T(4,128)}) custom-call(s32[4,8,10]{2,1,0:T(8,128)} %target_ref.3, s32[16]{0:T(128)} %order_ref.1, f32[8,40,128]{2,1,0:T(8,128)} %get-tuple-element.10.got_ref, f32[4,8,8,128]{3,2,1,0:T(8,128)} %get-tuple-element.11.all_ref), custom_call_target="tpu_custom_call" | custom-call | tf_op jit(solution)/shard_map/select/pallas_call | solution.py:499
Async XLA Ops:
  0.6 2.5 %copy-start = (bf16[10,32,64,128]{3,2,1,0:T(8,128)(2,1)S(1)}, bf16[10,32,64,128]{3,2,1,0:T(8,128)(2,1)}, u32[]{:S(2)}) copy-start(bf16[10,32,64,128]{3,2,1,0:T(8,128)(2,1)} %f_ref.3) | copy-start | bytes 15728644
  3.1 19.4 %copy-start.1 = (bf16[4,1536,256]{2,1,0:T(8,128)(2,1)S(1)}, bf16[4,1536,256]{2,1,0:T(8,128)(2,1)}, u32[]{:S(2)}) copy-start(bf16[4,1536,256]{2,1,0:T(8,128)(2,1)} %constant.4.clone.w_ref) | copy-start | bytes 9437188
  3.1 19.4 %copy-start.2 = (bf16[4096,128]{1,0:T(8,128)(2,1)S(1)}, bf16[4096,128]{1,0:T(8,128)(2,1)}, u32[]{:S(2)}) copy-start(bf16[4096,128]{1,0:T(8,128)(2,1)} %constant.5.clone.m_ref) | copy-start | bytes 3145732
  3.1 19.4 %copy-start.4 = (s32[4,8,10]{2,1,0:T(8,128)S(1)}, s32[4,8,10]{2,1,0:T(8,128)}, u32[]{:S(2)}) copy-start(s32[4,8,10]{2,1,0:T(8,128)} %target_ref.3) | copy-start | bytes 3844
  3.1 19.4 %copy-start.5 = (s32[4,8,10]{2,1,0:T(8,128)S(1)}, s32[4,8,10]{2,1,0:T(8,128)}, u32[]{:S(2)}) copy-start(s32[4,8,10]{2,1,0:T(8,128)} %list_ref.1) | copy-start | bytes 3844
  54.2 0.7 copy-start.3

commit v2 on v1

--- a/solution.py
+++ b/solution.py
@@ -69,15 +69,6 @@
         )
         copy.start()
         return copy
-
-    row = iota((2 * ny, 256), 0)
-    lane = iota((2 * ny, 256), 1)
-    y, l = row % ny, lane % 128
-    spot = l - row // ny * HW
-    low = jnp.where((lane < 128) & (y >= ny - HW), spot - y + (ny - HW), -1)
-    base = jnp.where((lane >= 128) & (y < HW), spot - y, low)
-    for j in range(nz // 2):
-        col[j] = one_hot(base == 2 * HW * j)
 
     def pack(ref, lo):
         acc = None
@@ -104,6 +95,15 @@
             block = f_ref[c, :, start : start + 16, :].reshape(nz * 16, ny)
             sx[side, c * hz : (c + 1) * hz, :] = dot(take, block).astype(BF)
         xcopies.append(send(sx.at[side], rx.at[side], side, who))
+    row = iota((2 * ny, 256), 0)
+    lane = iota((2 * ny, 256), 1)
+    y, l = row % ny, lane % 128
+    spot = l - row // ny * HW
+    low = jnp.where((lane < 128) & (y >= ny - HW), spot - y + (ny - HW), -1)
+    base = jnp.where((lane >= 128) & (y < HW), spot - y, low)
+    for j in range(nz // 2):
+        col[j] = one_hot(base == 2 * HW * j)
+
     for part in range(nx // 16):
         both = pack(f_ref, part * 16)
         for side in range(2):
@@ -153,6 +153,7 @@
     w_ref,
     m_ref,
     pay_ref,
+    co_ref,
     t_ref,
     qp_ref,
     qm_ref,
@@ -320,58 +321,47 @@
         placed = jnp.where(spot == 2 * row, even, jnp.where(spot == 2 * row + 1, odd, 0.0))
         sums = jnp.sum(placed, axis=0, keepdims=True) * (1.0 / 64.0)
         rows.append(sums / jnp.maximum(count_ref[cell, 0:1, :], 1.0))
-    coarse = jnp.concatenate(rows, axis=0)
-    for g in range(gxn):
-        pay_ref[g, CAP * 16 : CAP * 16 + cells, :] = coarse
-
-
-def exchange_kernel(gxn, gyn, pay_ref, got_ref, all_ref, mine, xs, xr, ys, yr):
+    co_ref[...] = jnp.concatenate(rows, axis=0)
+
+
+def exchange_kernel(
+    gxn, gyn, pay_ref, co_ref, got_ref, all_ref, xs, xr, ys, yr, zs, zr
+):
     gx, gy = lax.axis_index("gx"), lax.axis_index("gy")
+    row_peers = [(lax.rem(gx + d, gxn), gy) for d in range(1, gxn)]
+    column_peers = [(gx, lax.rem(gy + d, gyn)) for d in range(1, gyn)]
     barrier = pltpu.get_barrier_semaphore()
-    for d in range(1, gxn):
-        pl.semaphore_signal(
-            barrier, inc=1, device_id=(lax.rem(gx + d, gxn), gy), device_id_type=MESH
+    for who in row_peers + column_peers:
+        pl.semaphore_signal(barrier, inc=1, device_id=who, device_id_type=MESH)
+    pl.semaphore_wait(barrier, gxn + gyn - 2)
+
+    def send(src, dst, sends, receives, number, who):
+        copy = pltpu.make_async_remote_copy(
+            src_ref=src,
+            dst_ref=dst,
+            send_sem=sends.at[number],
+            recv_sem=receives.at[number],
+            device_id=who,
+            device_id_type=MESH,
         )
-    for d in range(1, gyn):
-        pl.semaphore_signal(
-            barrier, inc=1, device_id=(gx, lax.rem(gy + d, gyn)), device_id_type=MESH
-        )
-    pl.semaphore_wait(barrier, gxn + gyn - 2)
-    copies = []
-    for d in range(1, gxn):
-        who = lax.rem(gx + d, gxn)
-        copies.append(
-            pltpu.make_async_remote_copy(
-                src_ref=pay_ref.at[who],
-                dst_ref=got_ref.at[gx],
-                send_sem=xs.at[d],
-                recv_sem=xr.at[d],
-                device_id=(who, gy),
-                device_id_type=MESH,
-            )
-        )
-        copies[-1].start()
+        copy.start()
+        return copy
+
+    small = [
+        send(co_ref, all_ref.at[gx, gy], ys, yr, n, who) for n, who in enumerate(column_peers)
+    ]
+    large = [
+        send(pay_ref.at[who[0]], got_ref.at[gx], xs, xr, n, who)
+        for n, who in enumerate(row_peers)
+    ]
+    all_ref[gx, gy] = co_ref[...]
     got_ref[gx] = pay_ref[gx]
-    for copy in copies:
+    for copy in small:
         copy.wait()
-    cells = mine.shape[1]
-    for g in range(gxn):
-        mine[g] = got_ref[g, CAP * 16 : CAP * 16 + cells, :]
-    copies = []
-    for d in range(1, gyn):
-        copies.append(
-            pltpu.make_async_remote_copy(
-                src_ref=mine,
-                dst_ref=all_ref.at[gy],
-                send_sem=ys.at[d],
-                recv_sem=yr.at[d],
-                device_id=(gx, lax.rem(gy + d, gyn)),
-                device_id_type=MESH,
-            )
-        )
-        copies[-1].start()
-    all_ref[gy] = mine[...]
-    for copy in copies:
+    large = large + [
+        send(all_ref.at[gx], all_ref.at[gx], zs, zr, n, who) for n, who in enumerate(row_peers)
+    ]
+    for copy in large:
         copy.wait()
 
 
@@ -380,20 +370,18 @@
 ):
     gx, gy = lax.axis_index("gx"), lax.axis_index("gy")
 
+    spare = o_ref.shape[0]
+
     def source(s, slot):
         def entry(e, carry):
             slot, rank = carry
             hit = target_ref[gy, s, e] == gx
-
-            @pl.when(hit)
-            def _():
-                at = pl.multiple_of(rank * 16, 16)
-                held[slot] = got_ref[s, pl.ds(at, 16), :]
-
+            at = pl.multiple_of(jnp.minimum(rank, CAP - 1) * 16, 16)
+            held[jnp.where(hit, slot, spare)] = got_ref[s, pl.ds(at, 16), :]
             step = jnp.where(hit, 1, 0).astype(jnp.int32)
             return slot + step, rank + step
 
-        return lax.fori_loop(0, list_length, entry, (slot, jnp.int32(0)))[0]
+        return lax.fori_loop(0, list_length, entry, (slot, jnp.int32(0)), unroll=True)[0]
 
     lax.fori_loop(0, gxn, source, jnp.int32(0))
     for slot in range(o_ref.shape[0]):
@@ -410,7 +398,7 @@
             row = None
             for i in range(4):
                 cx = part * 4 + i
-                value = all_ref[owner, cx // cells_x, pl.ds(first + cx % cells_x, 1), :]
+                value = all_ref[cx // cells_x, owner, pl.ds(first + cx % cells_x, 1), :]
                 row = value if row is None else jnp.where(group == i, value, row)
             c_ref[r : r + 1, part * 128 : (part + 1) * 128] = row
 
@@ -449,11 +437,14 @@
         ),
         name="halo",
     )(fields)
-    payload = pl.pallas_call(
+    payload, own_cells = pl.pallas_call(
         functools.partial(tile_kernel, gxn, gyn, list_length),
-        out_shape=jax.ShapeDtypeStruct((gxn, CAP * 16 + cells, 128), F32),
+        out_shape=(
+            jax.ShapeDtypeStruct((gxn, CAP * 16, 128), F32),
+            jax.ShapeDtypeStruct((cells, 128), F32),
+        ),
         in_specs=[SM, SM] + [VM] * 6,
-        out_specs=VM,
+        out_specs=(VM, VM),
         scratch_shapes=[
             pltpu.VMEM((SPAN // 4, nc * 48, 128), F32),
             pltpu.VMEM((144, SPAN * 32), BF),
@@ -482,20 +473,21 @@
         functools.partial(exchange_kernel, gxn, gyn),
         out_shape=(
             jax.ShapeDtypeStruct(payload.shape, F32),
-            jax.ShapeDtypeStruct((gyn, gxn, cells, 128), F32),
+            jax.ShapeDtypeStruct((gxn, gyn, cells, 128), F32),
         ),
-        in_specs=[VM],
+        in_specs=[VM, VM],
         out_specs=(VM, VM),
         scratch_shapes=[
-            pltpu.VMEM((gxn, cells, 128), F32),
-            pltpu.SemaphoreType.DMA((gxn,)),
-            pltpu.SemaphoreType.DMA((gxn,)),
-            pltpu.SemaphoreType.DMA((gyn,)),
-            pltpu.SemaphoreType.DMA((gyn,)),
+            pltpu.SemaphoreType.DMA((gxn - 1,)),
+            pltpu.SemaphoreType.DMA((gxn - 1,)),
+            pltpu.SemaphoreType.DMA((gyn - 1,)),
+            pltpu.SemaphoreType.DMA((gyn - 1,)),
+            pltpu.SemaphoreType.DMA((gxn - 1,)),
+            pltpu.SemaphoreType.DMA((gxn - 1,)),
         ],
         compiler_params=pltpu.CompilerParams(collective_id=1, has_side_effects=True),
         name="exchange",
-    )(payload)
+    )(payload, own_cells)
     statistics, coarse = pl.pallas_call(
         functools.partial(select_kernel, gxn, gyn, list_length, cells_x),
         out_shape=(
@@ -504,7 +496,7 @@
         ),
         in_specs=[SM, SM, VM, VM],
         out_specs=(VM, VM),
-        scratch_shapes=[pltpu.VMEM((per_filter, 16, 128), F32)],
+        scratch_shapes=[pltpu.VMEM((per_filter + 1, 16, 128), F32)],
         name="select",
     )(filter_device, pencil_order, got, every)
     return statistics, coarse

time: 71.4 us -> 69.1 us (0.968); the launches traced: 71.3 us -> 68.3 us
  Pallas kernels: 67.5 us -> 63.9 us
    pallas_call x1, Pallas kernels: 31.7 us -> 7.43 us  [shards(): pl.pallas_call(functools.partial(tile_kernel, gxn, gyn, list_length), out...]
    pallas_call x1, Pallas kernels: 13.3 us -> 35 us  [shards(): pl.pallas_call(functools.partial(exchange_kernel, gxn, gyn), out_shape=(j...]
    pallas_call x1, Pallas kernels: 3.11 us -> 2.09 us  [shards(): pl.pallas_call(functools.partial(select_kernel, gxn, gyn, list_length, ce...]
    unnamed x12 -> x14, local copies, waits for them, and re-layouts: 3.14 us -> 3.73 us
where the time goes in v2:
time: 69.1 us; the launch traced here: 68.3 us
  Pallas kernels  63.9 us (92%)
  local copies, waits for them, and re-layouts  3.73 us (5%)
  between operations  0.7 us (1%)
    pallas_call x1, Pallas kernels, shards(): pl.pallas_call(functools.partial(exchange_kernel, gxn, gyn), out_shape=(j...  35 us
    pallas_call x1, Pallas kernels, shards(): pl.pallas_call(functools.partial(halo_kernel, gxn, gyn), out_shape=(jax.S...  19.4 us
    pallas_call x1, Pallas kernels, shards(): pl.pallas_call(functools.partial(tile_kernel, gxn, gyn, list_length), out...  7.43 us
    unnamed x14, local copies, waits for them, and re-layouts  3.73 us
    pallas_call x1, Pallas kernels, shards(): pl.pallas_call(functools.partial(select_kernel, gxn, gyn, list_length, ce...  2.09 us

profile of v2, /device:TPU:0, one launch (start us, length us, event | category | flops | bytes accessed | tf_op | source)
XLA Modules:
  0.0 68.3 jit_solution(10763109298566421494)
XLA Ops:
  0.6 0.0 copy-start
  0.6 2.5 %copy-done = bf16[10,32,64,128]{3,2,1,0:T(8,128)(2,1)S(1)} copy-done((bf16[10,32,64,128]{3,2,1,0:T(8,128)(2,1)S(1)}, bf16[10,32,64,128]{3,2,1,0:T(8,128)(2,1)}, u32[]{:S(2)}) %copy-start) | copy-done | bytes 5242904
  3.1 0.0 copy-start.1
  3.1 0.0 copy-start.2
  3.1 0.0 copy-start.4
  3.1 0.0 copy-start.5
  3.1 19.4 %halo.1 = (bf16[10,32,16,128]{3,2,1,0:T(8,128)(2,1)S(1)}, bf16[2,10,64,128]{3,2,1,0:T(8,128)(2,1)S(1)}, bf16[2,10,16,128]{3,2,1,0:T(8,128)(2,1)S(1)}) custom-call(bf16[10,32,64,128]{3,2,1,0:T(8,128)(2,1)S(1)} %copy-done), custom_call_target="tpu_custom_call" | custom-call | tf_op jit(solution)/shard_map/halo/pallas_call | solution.py:417
  22.5 0.0 copy-done.1
  22.5 0.0 copy-done.2
  22.5 0.0 copy-done.4
  22.5 0.0 copy-done.5
  22.5 7.4 %tiles.1 = (f32[8,32,128]{2,1,0:T(8,128)S(1)}, f32[8,128]{1,0:T(8,128)S(1)}) custom-call(s32[4,8,10]{2,1,0:T(8,128)S(1)} %copy-done.5, s32[4,8,10]{2,1,0:T(8,128)S(1)} %copy-done.4, bf16[10,32,64,128]{3,2,1,0:T(8,128)(2,1)S(1)} %copy-done, bf16[10,32,16,128]{3,2,1,0:T(8,128)(2,1)S(1)} %get-tuple-element.9.e_ref, ...), custom_call_target="tpu_custom_call" | custom-call | tf_op jit(solution)/shard_map/tiles/pallas_call | solution.py:440
  30.0 0.0 copy-start.3
  30.0 0.6 copy-done.3
  30.6 0.0 copy-start.6
  30.6 0.6 copy-done.6
  31.2 35.0 %exchange.1 = (f32[8,32,128]{2,1,0:T(8,128)}, f32[8,4,8,128]{3,2,1,0:T(8,128)}) custom-call(f32[8,32,128]{2,1,0:T(8,128)} %copy-done.3, f32[8,128]{1,0:T(8,128)} %copy-done.6), custom_call_target="tpu_custom_call" | custom-call | tf_op jit(solution)/shard_map/exchange/pallas_call | solution.py:472
  66.2 2.1 %select.1 = (f32[4,2048]{1,0:T(4,128)}, f32[4,512]{1,0:T(4,128)}) custom-call(s32[4,8,10]{2,1,0:T(8,128)} %target_ref.3, s32[16]{0:T(128)} %order_ref.1, f32[8,32,128]{2,1,0:T(8,128)} %get-tuple-element.14.got_ref, f32[8,4,8,128]{3,2,1,0:T(8,128)} %get-tuple-element.15.all_ref), custom_call_target="tpu_custom_call" | custom-call | tf_op jit(solution)/shard_map/select/pallas_call | solution.py:491
Async XLA Ops:
  0.6 2.5 %copy-start = (bf16[10,32,64,128]{3,2,1,0:T(8,128)(2,1)S(1)}, bf16[10,32,64,128]{3,2,1,0:T(8,128)(2,1)}, u32[]{:S(2)}) copy-start(bf16[10,32,64,128]{3,2,1,0:T(8,128)(2,1)} %f_ref.3) | copy-start | bytes 15728644
  3.1 19.4 %copy-start.1 = (bf16[4,1536,256]{2,1,0:T(8,128)(2,1)S(1)}, bf16[4,1536,256]{2,1,0:T(8,128)(2,1)}, u32[]{:S(2)}) copy-start(bf16[4,1536,256]{2,1,0:T(8,128)(2,1)} %constant.4.clone.w_ref) | copy-start | bytes 9437188
  3.1 19.4 %copy-start.2 = (bf16[4096,128]{1,0:T(8,128)(2,1)S(1)}, bf16[4096,128]{1,0:T(8,128)(2,1)}, u32[]{:S(2)}) copy-start(bf16[4096,128]{1,0:T(8,128)(2,1)} %constant.5.clone.m_ref) | copy-start | bytes 3145732
  3.1 19.4 %copy-start.4 = (s32[4,8,10]{2,1,0:T(8,128)S(1)}, s32[4,8,10]{2,1,0:T(8,128)}, u32[]{:S(2)}) copy-start(s32[4,8,10]{2,1,0:T(8,128)} %target_ref.3) | copy-start | bytes 3844
  3.1 19.4 %copy-start.5 = (s32[4,8,10]{2,1,0:T(8,128)S(1)}, s32[4,8,10]{2,1,0:T(8,128)}, u32[]{:S(2)}) copy-start(s32[4,8,10]{2,1,0:T(8,128)} %list_ref.1) | copy-start | bytes 3844
  30.0 0.6 copy-start.3
  30.6 0.6 copy-start.6

commit v3 on v2

--- a/solution.py
+++ b/solution.py
@@ -70,17 +70,17 @@
         copy.start()
         return copy
 
-    def pack(ref, lo):
+    def pack(ref, lo, rows):
         acc = None
         for j in range(nz // 2):
             lhs = jnp.concatenate(
-                [ref[:, 2 * j + i, lo : lo + 16, :].reshape(nc * 16, ny) for i in range(2)],
+                [ref[:, 2 * j + i, lo : lo + rows, :].reshape(nc * rows, ny) for i in range(2)],
                 axis=1,
             )
             part = dot(lhs, col[j])
             acc = part if acc is None else acc + part
         return [
-            acc[:, side * 128 : (side + 1) * 128].astype(BF).reshape(nc, 16, 128)
+            acc[:, side * 128 : (side + 1) * 128].astype(BF).reshape(nc, rows, 128)
             for side in range(2)
         ]
 
@@ -104,10 +104,10 @@
     for j in range(nz // 2):
         col[j] = one_hot(base == 2 * HW * j)
 
-    for part in range(nx // 16):
-        both = pack(f_ref, part * 16)
+    for part in range(nx // 32):
+        both = pack(f_ref, part * 32, 32)
         for side in range(2):
-            sy[side, :, part * 16 : part * 16 + 16, :] = both[side]
+            sy[side, :, part * 32 : part * 32 + 32, :] = both[side]
     ycopies = [send(sy.at[0], yh_ref.at[0], 2, up), send(sy.at[1], yh_ref.at[1], 3, down)]
     put = iota((nz * 16, 2 * hz), 0)
     src = iota((nz * 16, 2 * hz), 1)
@@ -123,7 +123,7 @@
         rows = slice(c * hz, (c + 1) * hz)
         block = dot(give, jnp.concatenate([rx[0, rows, :], rx[1, rows, :]], axis=0))
         e_ref[c] = block.astype(BF).reshape(nz, 16, ny)
-    both = pack(e_ref, 0)
+    both = pack(e_ref, 0, 16)
     for side in range(2):
         sc[side] = both[side]
     ycopies.append(send(sc.at[0], yc_ref.at[0], 4, up))

time: 69.1 us -> 70.2 us (1.016)
  Pallas kernels: 63.9 us -> 65.1 us
where the time goes in v3:
time: 70.2 us; the launch traced here: 69.6 us
  Pallas kernels  65.1 us (93%)
  local copies, waits for them, and re-layouts  3.73 us (5%)
    pallas_call x1, Pallas kernels, shards(): pl.pallas_call(functools.partial(exchange_kernel, gxn, gyn), out_shape=(j...  35.6 us
    pallas_call x1, Pallas kernels, shards(): pl.pallas_call(functools.partial(halo_kernel, gxn, gyn), out_shape=(jax.S...  19.4 us
    pallas_call x1, Pallas kernels, shards(): pl.pallas_call(functools.partial(tile_kernel, gxn, gyn, list_length), out...  8.07 us
    unnamed x14, local copies, waits for them, and re-layouts  3.73 us
    pallas_call x1, Pallas kernels, shards(): pl.pallas_call(functools.partial(select_kernel, gxn, gyn, list_length, ce...  2.09 us

profile of v3, /device:TPU:0, one launch (start us, length us, event | category | flops | bytes accessed | tf_op | source)
XLA Modules:
  0.0 69.6 jit_solution(13842867195842536205)
XLA Ops:
  0.6 0.0 copy-start
  0.6 2.5 %copy-done = bf16[10,32,64,128]{3,2,1,0:T(8,128)(2,1)S(1)} copy-done((bf16[10,32,64,128]{3,2,1,0:T(8,128)(2,1)S(1)}, bf16[10,32,64,128]{3,2,1,0:T(8,128)(2,1)}, u32[]{:S(2)}) %copy-start) | copy-done | bytes 5242904
  3.1 0.0 copy-start.1
  3.1 0.0 copy-start.2
  3.1 0.0 copy-start.4
  3.1 0.0 copy-start.5
  3.1 19.4 %halo.1 = (bf16[10,32,16,128]{3,2,1,0:T(8,128)(2,1)S(1)}, bf16[2,10,64,128]{3,2,1,0:T(8,128)(2,1)S(1)}, bf16[2,10,16,128]{3,2,1,0:T(8,128)(2,1)S(1)}) custom-call(bf16[10,32,64,128]{3,2,1,0:T(8,128)(2,1)S(1)} %copy-done), custom_call_target="tpu_custom_call" | custom-call | tf_op jit(solution)/shard_map/halo/pallas_call | solution.py:417
  22.5 0.0 copy-done.1
  22.5 0.0 copy-done.2
  22.5 0.0 copy-done.4
  22.5 0.0 copy-done.5
  22.5 8.1 %tiles.1 = (f32[8,32,128]{2,1,0:T(8,128)S(1)}, f32[8,128]{1,0:T(8,128)S(1)}) custom-call(s32[4,8,10]{2,1,0:T(8,128)S(1)} %copy-done.5, s32[4,8,10]{2,1,0:T(8,128)S(1)} %copy-done.4, bf16[10,32,64,128]{3,2,1,0:T(8,128)(2,1)S(1)} %copy-done, bf16[10,32,16,128]{3,2,1,0:T(8,128)(2,1)S(1)} %get-tuple-element.9.e_ref, ...), custom_call_target="tpu_custom_call" | custom-call | tf_op jit(solution)/shard_map/tiles/pallas_call | solution.py:440
  30.6 0.0 copy-start.3
  30.6 0.6 copy-done.3
  31.3 0.0 copy-start.6
  31.3 0.6 copy-done.6
  31.9 35.6 %exchange.1 = (f32[8,32,128]{2,1,0:T(8,128)}, f32[8,4,8,128]{3,2,1,0:T(8,128)}) custom-call(f32[8,32,128]{2,1,0:T(8,128)} %copy-done.3, f32[8,128]{1,0:T(8,128)} %copy-done.6), custom_call_target="tpu_custom_call" | custom-call | tf_op jit(solution)/shard_map/exchange/pallas_call | solution.py:472
  67.5 2.1 %select.1 = (f32[4,2048]{1,0:T(4,128)}, f32[4,512]{1,0:T(4,128)}) custom-call(s32[4,8,10]{2,1,0:T(8,128)} %target_ref.3, s32[16]{0:T(128)} %order_ref.1, f32[8,32,128]{2,1,0:T(8,128)} %get-tuple-element.14.got_ref, f32[8,4,8,128]{3,2,1,0:T(8,128)} %get-tuple-element.15.all_ref), custom_call_target="tpu_custom_call" | custom-call | tf_op jit(solution)/shard_map/select/pallas_call | solution.py:491
Async XLA Ops:
  0.6 2.5 %copy-start = (bf16[10,32,64,128]{3,2,1,0:T(8,128)(2,1)S(1)}, bf16[10,32,64,128]{3,2,1,0:T(8,128)(2,1)}, u32[]{:S(2)}) copy-start(bf16[10,32,64,128]{3,2,1,0:T(8,128)(2,1)} %f_ref.3) | copy-start | bytes 15728644
  3.1 19.4 %copy-start.1 = (bf16[4,1536,256]{2,1,0:T(8,128)(2,1)S(1)}, bf16[4,1536,256]{2,1,0:T(8,128)(2,1)}, u32[]{:S(2)}) copy-start(bf16[4,1536,256]{2,1,0:T(8,128)(2,1)} %constant.4.clone.w_ref) | copy-start | bytes 9437188
  3.1 19.4 %copy-start.2 = (bf16[4096,128]{1,0:T(8,128)(2,1)S(1)}, bf16[4096,128]{1,0:T(8,128)(2,1)}, u32[]{:S(2)}) copy-start(bf16[4096,128]{1,0:T(8,128)(2,1)} %constant.5.clone.m_ref) | copy-start | bytes 3145732
  3.1 19.4 %copy-start.4 = (s32[4,8,10]{2,1,0:T(8,128)S(1)}, s32[4,8,10]{2,1,0:T(8,128)}, u32[]{:S(2)}) copy-start(s32[4,8,10]{2,1,0:T(8,128)} %target_ref.3) | copy-start | bytes 3844
  3.1 19.4 %copy-start.5 = (s32[4,8,10]{2,1,0:T(8,128)S(1)}, s32[4,8,10]{2,1,0:T(8,128)}, u32[]{:S(2)}) copy-start(s32[4,8,10]{2,1,0:T(8,128)} %list_ref.1) | copy-start | bytes 3844
  30.6 0.6 copy-start.3
  31.3 0.6 copy-start.6
